TPU v7x, 32 devices: a whole 2x2x4 slice. The times are simulated.
32 devices in a mesh: bevy: 4 (over y, x), bevx: 4 (over z), cam: 2 (over core).
Axes of the slice: x: 2, y: 2, z: 4, core: 2. Of those that a mesh axis runs over, the one named last changes fastest.
Arguments:
- image_tokens: bfloat16 [8192, 768], P(('bevy', 'bevx', 'cam')), may hold values from -6 to 6
- lift_weight: bfloat16 [768, 1024], replicated, may hold values from -0.21875 to 0.21875
- route_token: int32 [16, 2, 16, 8], P(('bevy', 'bevx'), 'cam'), may hold values from 0 to 255
- route_cell: int32 [16, 2, 16, 8], P(None, 'cam', ('bevy', 'bevx')), may hold values from 0 to 1023
- slot_counts: int32 [16, 2, 16], P(('bevy', 'bevx'), 'cam'), may hold values from 0 to 8, as said below
- norm_gain: float32 [1024], replicated, may hold values from 0.1 to 1.9
- w_query: bfloat16 [1024, 1024], replicated, may hold values from -0.1875 to 0.1875
- w_key: bfloat16 [1024, 1024], replicated, may hold values from -0.1875 to 0.1875
- w_value: bfloat16 [1024, 1024], replicated, may hold values from -0.1875 to 0.1875
- w_out: bfloat16 [1024, 1024], replicated, may hold values from -0.1875 to 0.1875
- key_bias: bfloat16 [64, 256, 16], P(None, 'bevx'), may hold values from -1.5 to 260
Outputs:
- bev_out: bfloat16 [64, 256, 1024], P(('bevy', 'cam'), 'bevx')
Inputs may be any that keep to these rules, and one draw needn't show every extreme that they name: The first slot_counts slots of a source device and tile are live; at most 8. In every draw some tile receives 8 live slots from every source device.
All inputs are finite; a program needn't handle non-finite values.
Results may differ from a plain program's by a relative error of at most 0.0055.
Values may be sent and summed in bfloat16 or wider, within the bound.
A program may use at most 128 MiB of HBM per device.

v0:
```python
import jax
import jax.numpy as jnp
from jax import lax
from jax.sharding import PartitionSpec as P

ROWS_DEV = 8
COLS_DEV = 64
HALO = 4


def extended_2(cells, sides, width):
    for axis, dim in sides:
        count = lax.axis_size(axis)
        ends = count - 1
        head = lax.slice_in_dim(cells, 0, width, axis=dim)
        tail = lax.slice_in_dim(cells, cells.shape[dim] - width, cells.shape[dim], axis=dim)
        cells = jnp.concatenate(
            [
                lax.ppermute(tail, axis, [(i, (i + 1) % count) for i in range(ends)]),
                cells,
                lax.ppermute(head, axis, [((i + 1) % count, i) for i in range(ends)]),
            ],
            axis=dim,
        )
    return cells


def body(
    image_tokens,
    lift_weight,
    route_token,
    route_cell,
    slot_counts,
    norm_gain,
    w_query,
    w_key,
    w_value,
    w_out,
    key_bias,
):
    tile_count = route_token.shape[2]
    slot_count = route_token.shape[3]
    width_out = lift_weight.shape[1]
    head_count = key_bias.shape[2]
    head_size = width_out // head_count
    grid_rows = key_bias.shape[0]
    own_cells = ROWS_DEV * COLS_DEV
    is_live = (
        lax.broadcasted_iota(jnp.int32, (tile_count, slot_count), 1) < slot_counts[0, 0][:, None]
    )
    token_index = route_token[0, 0]
    projected = jnp.dot(image_tokens, lift_weight, preferred_element_type=jnp.float32).astype(
        jnp.bfloat16
    )
    picked = jnp.where(is_live[:, :, None], projected[token_index], jnp.zeros((), jnp.bfloat16))
    arrived = lax.all_to_all(picked, ("bevy", "bevx"), split_axis=0, concat_axis=0, tiled=True)
    arrived_rows = arrived.reshape(tile_count * slot_count, -1)
    cell_index = route_cell[:, 0, 0, :].reshape(-1)
    both_rows, both_cells = (
        lax.all_gather(arrived_rows, "cam", axis=0, tiled=True),
        lax.all_gather(cell_index, "cam", axis=0, tiled=True),
    )
    first_cell = lax.axis_index("cam") * own_cells
    cell_ids = first_cell + lax.broadcasted_iota(jnp.int32, (own_cells, both_cells.shape[0]), 0)
    one_hot = (cell_ids == both_cells[None, :]).astype(jnp.bfloat16)
    lifted = jnp.dot(one_hot, both_rows, preferred_element_type=jnp.float32)
    mean_square = jnp.mean(lifted * lifted, axis=-1, keepdims=True)
    normed = (lifted * lax.rsqrt(mean_square + 1e-06) * norm_gain).astype(jnp.bfloat16)
    queries = jnp.dot(normed, w_query, preferred_element_type=jnp.float32).astype(jnp.bfloat16)
    row_start = lax.axis_index(("bevy", "cam")) * ROWS_DEV
    key_local = jnp.dot(normed, w_key, preferred_element_type=jnp.float32).astype(jnp.bfloat16)
    value_local = jnp.dot(normed, w_value, preferred_element_type=jnp.float32).astype(jnp.bfloat16)
    stacked = jnp.concatenate([key_local, value_local], axis=-1).reshape(
        ROWS_DEV, COLS_DEV, 2 * width_out
    )
    extended = extended_2(stacked, ((("bevy", "cam"), 0),), HALO).reshape(-1, 2 * width_out)
    key_vectors = extended[:, :width_out]
    value_vectors = extended[:, width_out:]
    bias_padded = jnp.pad(key_bias, ((HALO, HALO), (0, 0), (0, 0)))
    bias_rows = (
        lax.dynamic_slice_in_dim(bias_padded, row_start, 2 * ROWS_DEV, 0)
        .reshape(-1, head_count)
        .astype(jnp.float32)
    )
    key_row = row_start - HALO + jnp.arange(2 * ROWS_DEV, dtype=jnp.int32)
    key_valid = jnp.repeat((key_row >= 0) & (key_row < grid_rows), COLS_DEV)
    query_heads = queries.reshape(own_cells, head_count, head_size)
    key_heads = key_vectors.reshape(-1, head_count, head_size)
    value_heads = value_vectors.reshape(-1, head_count, head_size)
    score_scale = head_size ** (-0.5)
    scores = (
        jnp.einsum("qhd,khd->hqk", query_heads, key_heads, preferred_element_type=jnp.float32)
        * score_scale
    )
    scores = scores + bias_rows.T[:, None, :]
    scores = jnp.where(key_valid[None, None, :], scores, -jnp.inf)
    top_score = jnp.max(scores, axis=-1, keepdims=True)
    expo = jnp.exp(scores - top_score)
    weights = (expo / jnp.sum(expo, axis=-1, keepdims=True)).astype(jnp.bfloat16)
    attended = jnp.einsum(
        "hqk,khd->qhd", weights, value_heads, preferred_element_type=jnp.float32
    ).astype(jnp.bfloat16)
    attended = attended.reshape(own_cells, width_out)
    result = lifted + jnp.dot(attended, w_out, preferred_element_type=jnp.float32)
    return result.astype(jnp.bfloat16).reshape(ROWS_DEV, COLS_DEV, width_out)


def solution(mesh):
    placed = (
        P(("bevy", "bevx", "cam"), None),
        P(),
        P(("bevy", "bevx"), "cam", None, None),
        P(None, "cam", ("bevy", "bevx"), None),
        P(("bevy", "bevx"), "cam", None),
        P(),
        P(),
        P(),
        P(),
        P(),
        P(None, "bevx", None),
    )
    return jax.shard_map(
        body,
        mesh=mesh,
        in_specs=placed,
        out_specs=P(("bevy", "cam"), "bevx", None),
        check_vma=False,
    )
```

profile of v0, /device:TPU:1, one launch (start us, length us, event | category | flops | bytes accessed | tf_op | source)
XLA Modules:
  0.0 104.2 jit_solution(2424097182725678871)
XLA Ops:
  0.0 0.9 iota_compare_fusion
  1.7 2.1 %convolution_convert_fusion.3 = bf16[256,1024]{1,0:T(8,128)(2,1)S(1)} fusion(bf16[256,768]{1,0:T(8,128)(2,1)} %param.11, bf16[768,1024]{1,0:T(8,128)(2,1)} %param.12), kind=kOutput, calls=%fused_computation.24 | convolution fusion | flops 402915328 | bytes 2490368 | tf_op jit(solution)/shard_map/dot_general | solution.py:52
  3.9 0.9 gather_fusion
  5.5 7.5 %all-to-all-start = ((bf16[16,8,1024]{2,1,0:T(8,128)(2,1)}), bf16[16,8,1024]{2,1,0:T(8,128)(2,1)S(1)}, u32[]{:S(2)}, u32[]{:S(2)}) async-start(bf16[16,8,1024]{2,1,0:T(8,128)(2,1)} %bitcast_select_fusion), calls=%async_computation | async-start | bytes 524288 | tf_op jit(solution)/shard_map/all_to_all | solution.py:56
  13.3 2.4 %all-gather = s32[2,1,128]{2,1,0:T(1,128)S(1)} all-gather(s32[1,1,128]{2,1,0:T(1,128)S(1)} %reshape.111), channel_id=1, replica_groups=mesh['bevy'=4,'bevx'=4,'cam'=2] {'cam'}, dimensions={0}, use_global_device_ids=true | all-gather | bytes 1536 | tf_op jit(solution)/shard_map/all_gather | solution.py:61
  15.7 6.6 %all-to-all-done = bf16[16,8,1024]{2,1,0:T(8,128)(2,1)S(1)} async-done(((bf16[16,8,1024]{2,1,0:T(8,128)(2,1)}), bf16[16,8,1024]{2,1,0:T(8,128)(2,1)S(1)}, u32[]{:S(2)}, u32[]{:S(2)}) %all-to-all-start) | async-done | bytes 262176 | tf_op jit(solution)/shard_map/all_to_all | solution.py:56
  22.3 4.1 %all_gather.7 = bf16[256,1024]{1,0:T(8,128)(2,1)S(1)} all-gather(bf16[128,1024]{1,0:T(8,128)(2,1)S(1)} %bitcast.47), channel_id=1, replica_groups=mesh['bevy'=4,'bevx'=4,'cam'=2] {'cam'}, dimensions={0}, use_global_device_ids=true | all-gather | bytes 786432 | tf_op jit(solution)/shard_map/all_gather | solution.py:60
  27.3 1.3 %convolution_convert_fusion.1 = bf16[512,1024]{1,0:T(8,128)(2,1)S(1)} fusion(bf16[512,1024]{1,0:T(8,128)(2,1)S(1)} %multiply_convert_fusion, bf16[1024,1024]{1,0:T(8,128)(2,1)S(1)} %copy-done), kind=kOutput, calls=%fused_computation.21 | convolution fusion | flops 1074266112 | bytes 4194304 | tf_op jit(solution)/shard_map/dot_general | solution.py:72
  28.6 1.1 %copy-done.11 = bf16[1024,1024]{1,0:T(8,128)(2,1)S(1)} copy-done((bf16[1024,1024]{1,0:T(8,128)(2,1)S(1)}, bf16[1024,1024]{1,0:T(8,128)(2,1)}, u32[]{:S(2)}) %copy-start.11) | copy-done | bytes 2097176
  29.7 1.3 %convolution_convert_fusion.2 = bf16[512,1024]{1,0:T(8,128)(2,1)S(1)} fusion(bf16[512,1024]{1,0:T(8,128)(2,1)S(1)} %multiply_convert_fusion, bf16[1024,1024]{1,0:T(8,128)(2,1)S(1)} %copy-done.11), kind=kOutput, calls=%fused_computation.22 | convolution fusion | flops 1074266112 | bytes 4194304 | tf_op jit(solution)/shard_map/dot_general | solution.py:71
  31.0 1.5 %fusion.8 = (bf16[256,2048]{1,0:T(8,128)(2,1)}, bf16[256,2048]{1,0:T(8,128)(2,1)}) fusion(bf16[512,1024]{1,0:T(8,128)(2,1)S(1)} %convolution_convert_fusion.2, bf16[512,1024]{1,0:T(8,128)(2,1)S(1)} %convolution_convert_fusion.1), kind=kLoop, calls=%fused_computation.25 | loop fusion | flops 4194304 | bytes 4194304 | tf_op jit(solution)/shard_map/concatenate | solution.py:73
  32.7 2.3 %collective-permute-start.1 = (bf16[4,64,2048]{2,1,0:T(8,128)(2,1)}, bf16[4,64,2048]{2,1,0:T(8,128)(2,1)}, u32[]{:S(2)}, u32[]{:S(2)}) collective-permute-start(bf16[4,64,2048]{2,1,0:T(8,128)(2,1)} %bitcast.7), channel_id=1, source_target_pairs={{1,0},{8,1},{9,8},{16,9},{17,16},{24,17},{25,24},{3,2},{10,3},{11,... | collective-permute-start | bytes 3145736 | tf_op jit(solution)/shard_map/ppermute | solution.py:21
  34.9 3.5 %collective-permute-start = (bf16[4,64,2048]{2,1,0:T(8,128)(2,1)}, bf16[4,64,2048]{2,1,0:T(8,128)(2,1)}, u32[]{:S(2)}, u32[]{:S(2)}) collective-permute-start(bf16[4,64,2048]{2,1,0:T(8,128)(2,1)} %bitcast.5), channel_id=1, source_target_pairs={{0,1},{1,8},{8,9},{9,16},{16,17},{17,24},{24,25},{2,3},{3,10},{10,... | collective-permute-start | bytes 3145736 | tf_op jit(solution)/shard_map/ppermute | solution.py:19
  38.8 2.8 %convolution_convert_fusion = bf16[512,1024]{1,0:T(8,128)(2,1)S(1)} fusion(bf16[512,1024]{1,0:T(8,128)(2,1)S(1)} %copy-done.6, bf16[1024,1024]{1,0:T(8,128)(2,1)} %param.17), kind=kOutput, calls=%fused_computation.20 | convolution fusion | flops 1074266112 | bytes 4194304 | tf_op jit(solution)/shard_map/dot_general | solution.py:69
  41.7 1.3 %copy.26 = bf16[512,1024]{0,1:T(8,128)(2,1)} copy(bf16[512,1024]{1,0:T(8,128)(2,1)S(1)} %convolution_convert_fusion) | data formatting | bytes 2097152 | tf_op jit(solution)/shard_map/convert_element_type | solution.py:69
  43.0 1.4 %pad_maximum_fusion.1 = bf16[512,2048]{1,0:T(8,128)(2,1)S(1)} fusion(bf16[512,1024]{1,0:T(8,128)(2,1)S(1)} %convolution_convert_fusion.1, bf16[512,1024]{1,0:T(8,128)(2,1)} %copy-done.3), kind=kLoop, calls=%fused_computation.14 | loop fusion | flops 4194304 | bytes 4194304 | tf_op jit(solution)/shard_map/concatenate | solution.py:73
  44.4 13.9 %collective-permute-done.1 = bf16[4,64,2048]{2,1,0:T(8,128)(2,1)} collective-permute-done((bf16[4,64,2048]{2,1,0:T(8,128)(2,1)}, bf16[4,64,2048]{2,1,0:T(8,128)(2,1)}, u32[]{:S(2)}, u32[]{:S(2)}) %collective-permute-start.1) | collective-permute-done | bytes 1048608 | tf_op jit(solution)/shard_map/ppermute | solution.py:21
  58.4 1.8 %pad_maximum_fusion = bf16[16,64,2048]{2,1,0:T(8,128)(2,1)S(1)} fusion(bf16[4,64,2048]{2,1,0:T(8,128)(2,1)} %collective-permute-done.1, bf16[8,64,2048]{2,1,0:T(8,128)(2,1)S(1)} %bitcast.44, bf16[4,64,2048]{2,1,0:T(8,128)(2,1)} %collective-permute-done), kind=kLoop, calls=%fused_computation.11 | loop fusion | flops 4194304 | bytes 8388608 | tf_op jit(solution)/shard_map/concatenate | solution.py:17
  60.1 1.8 %fusion.19 = (bf16[1024,1024]{1,0:T(8,128)(2,1)}, bf16[1024,1024]{1,0:T(8,128)(2,1)S(1)}) fusion(bf16[1024,2048]{1,0:T(8,128)(2,1)S(1)} %bitcast.43), kind=kLoop, calls=%fused_computation.43 | loop fusion | bytes 8388608 | tf_op jit(solution)/shard_map/slice | solution.py:77
  61.9 3.9 %copy.30 = bf16[1024,1024]{0,1:T(8,128)(2,1)} copy(bf16[1024,1024]{1,0:T(8,128)(2,1)} %get-tuple-element.5) | data formatting | bytes 4194304
  65.9 2.5 %copy.29 = bf16[1024,1024]{0,1:T(8,128)(2,1)} copy(bf16[1024,1024]{1,0:T(8,128)(2,1)S(1)} %get-tuple-element.6) | data formatting | bytes 4194304
  68.4 17.9 %fusion.20 = (f32[16,512]{1,0:T(8,128)S(1)}, f32[16,512,1024]{2,1,0:T(8,128)}) fusion(f32[16,1024]{1,0:T(8,128)S(1)} %bitcast.49, pred[1024]{0:T(1024)(128)(4,1)S(1)} %broadcast_in_dim.40, bf16[512,16,64]{0,2,1:T(8,128)(2,1)S(1)} %bitcast.48, bf16[1024,16,64]{0,2,1:T(8,128)(2,1)} %bitcast.45), kind=kOutput, calls=%fused_computation.44 | convolution fusion | flops 1115685888 | bytes 36799488 | tf_op jit(solution)/shard_map/sub | solution.py:98
  86.3 13.3 %fusion.7 = bf16[16,64,512]{2,1,0:T(8,128)(2,1)S(1)} fusion(bf16[1024,16,64]{0,2,1:T(8,128)(2,1)S(1)} %bitcast.46, f32[16,512,1024]{2,1,0:T(8,128)} %get-tuple-element.12, f32[16,512]{1,0:T(8,128)S(1)} %get-tuple-element.11), kind=kOutput, calls=%fused_computation.23 | convolution fusion | flops 1091043328 | bytes 36732928 | tf_op jit(solution)/shard_map/hqk,khd->qhd/dot_general | solution.py:100
  99.6 4.6 %add_convert_fusion = bf16[512,1024]{1,0:T(8,128)(2,1)} fusion(f32[512,1024]{1,0:T(8,128)} %copy-done.2, bf16[512,1024]{0,1:T(8,128)(2,1)S(1)} %bitcast.52, bf16[1024,1024]{1,0:T(8,128)(2,1)} %param.20), kind=kOutput, calls=%fused_computation.17 | convolution fusion | flops 1074790400 | bytes 6291456 | tf_op jit(solution)/shard_map/dot_general | solution.py:104
  (41 shorter events, 3.3 us)
Async XLA Ops:
  0.0 27.3 %copy-start = (bf16[1024,1024]{1,0:T(8,128)(2,1)S(1)}, bf16[1024,1024]{1,0:T(8,128)(2,1)}, u32[]{:S(2)}) copy-start(bf16[1024,1024]{1,0:T(8,128)(2,1)} %param.19) | copy-start | bytes 6291460
  3.9 9.2 %copy-start.10 = (s32[16,1,1,8]{0,3,2,1:T(8,128)S(1)}, s32[16,1,1,8]{0,3,2,1:T(8,128)}, u32[]{:S(2)}) copy-start(s32[16,1,1,8]{0,3,2,1:T(8,128)} %param.14) | copy-start | bytes 1540
  5.5 21.5 %copy-start.9 = (f32[1024]{0:T(1024)S(1)}, f32[1024]{0:T(1024)}, u32[]{:S(2)}) copy-start(f32[1024]{0:T(1024)} %param.16) | copy-start | bytes 12292
  5.5 16.8 %all-to-all-start = ((bf16[16,8,1024]{2,1,0:T(8,128)(2,1)}), bf16[16,8,1024]{2,1,0:T(8,128)(2,1)S(1)}, u32[]{:S(2)}, u32[]{:S(2)}) async-start(bf16[16,8,1024]{2,1,0:T(8,128)(2,1)} %bitcast_select_fusion), calls=%async_computation | async-start | bytes 524288 | tf_op jit(solution)/shard_map/all_to_all | solution.py:56
  27.0 1.6 %copy-start.2 = (f32[512,1024]{1,0:T(8,128)}, f32[512,1024]{1,0:T(8,128)S(1)}, u32[]{:S(2)}) copy-start(f32[512,1024]{1,0:T(8,128)S(1)} %get-tuple-element.10) | copy-start | bytes 6291460
  27.3 1.4 %copy-start.5 = (bf16[512,1024]{1,0:T(8,128)(2,1)}, bf16[512,1024]{1,0:T(8,128)(2,1)S(1)}, u32[]{:S(2)}) copy-start(bf16[512,1024]{1,0:T(8,128)(2,1)S(1)} %multiply_convert_fusion) | copy-start | bytes 3145732
  27.3 2.4 %copy-start.11 = (bf16[1024,1024]{1,0:T(8,128)(2,1)S(1)}, bf16[1024,1024]{1,0:T(8,128)(2,1)}, u32[]{:S(2)}) copy-start(bf16[1024,1024]{1,0:T(8,128)(2,1)} %param.18) | copy-start | bytes 6291460
  31.0 1.7 %copy-start.3 = (bf16[512,1024]{1,0:T(8,128)(2,1)}, bf16[512,1024]{1,0:T(8,128)(2,1)S(1)}, u32[]{:S(2)}) copy-start(bf16[512,1024]{1,0:T(8,128)(2,1)S(1)} %convolution_convert_fusion.2) | copy-start | bytes 3145732
  31.0 7.6 %copy-start.8 = (bf16[64,64,16]{1,2,0:T(8,128)(2,1)S(1)}, bf16[64,64,16]{1,2,0:T(8,128)(2,1)}, u32[]{:S(2)}) copy-start(bf16[64,64,16]{1,2,0:T(8,128)(2,1)} %param.21) | copy-start | bytes 393220
  31.0 7.8 %copy-start.6 = (bf16[512,1024]{1,0:T(8,128)(2,1)S(1)}, bf16[512,1024]{1,0:T(8,128)(2,1)}, u32[]{:S(2)}) copy-start(bf16[512,1024]{1,0:T(8,128)(2,1)} %copy-done.5) | copy-start | bytes 3145732
  32.7 25.7 %collective-permute-start.1 = (bf16[4,64,2048]{2,1,0:T(8,128)(2,1)}, bf16[4,64,2048]{2,1,0:T(8,128)(2,1)}, u32[]{:S(2)}, u32[]{:S(2)}) collective-permute-start(bf16[4,64,2048]{2,1,0:T(8,128)(2,1)} %bitcast.7), channel_id=1, source_target_pairs={{1,0},{8,1},{9,8},{16,9},{17,16},{24,17},{25,24},{3,2},{10,3},{11,... | collective-permute-start | bytes 3145736 | tf_op jit(solution)/shard_map/ppermute | solution.py:21
  34.9 23.4 %collective-permute-start = (bf16[4,64,2048]{2,1,0:T(8,128)(2,1)}, bf16[4,64,2048]{2,1,0:T(8,128)(2,1)}, u32[]{:S(2)}, u32[]{:S(2)}) collective-permute-start(bf16[4,64,2048]{2,1,0:T(8,128)(2,1)} %bitcast.5), channel_id=1, source_target_pairs={{0,1},{1,8},{8,9},{9,16},{16,17},{17,24},{24,25},{2,3},{3,10},{10,... | collective-permute-start | bytes 3145736 | tf_op jit(solution)/shard_map/ppermute | solution.py:19
  65.9 2.5 %copy-start.7 = (bf16[512,1024]{0,1:T(8,128)(2,1)S(1)}, bf16[512,1024]{0,1:T(8,128)(2,1)}, u32[]{:S(2)}) copy-start(bf16[512,1024]{0,1:T(8,128)(2,1)} %copy.26) | copy-start | bytes 3145732
  68.4 17.9 %copy-start.4 = (bf16[1024,1024]{0,1:T(8,128)(2,1)S(1)}, bf16[1024,1024]{0,1:T(8,128)(2,1)}, u32[]{:S(2)}) copy-start(bf16[1024,1024]{0,1:T(8,128)(2,1)} %copy.29) | copy-start | bytes 6291460
  99.6 4.6 %copy-start.1 = (bf16[1024,1024]{1,0:T(8,128)(2,1)S(1)}, bf16[1024,1024]{1,0:T(8,128)(2,1)}, u32[]{:S(2)}) copy-start(bf16[1024,1024]{1,0:T(8,128)(2,1)} %param.19) | copy-start | bytes 6291460
where the time goes:
time: 106 us; the launch traced here: 104 us
  matrix products  43.9 us (41%)
  waiting for transfers between devices  20.6 us (19%)
  starting transfers between devices  13.3 us (13%)
  local copies, waits for them, and re-layouts  12.4 us (12%)
  other arithmetic  7.35 us (7%)
  blocking collectives  6.52 us (6%)
    sub x1, matrix products, body(): expo = jnp.exp(scores - top_score)  17.9 us
    ppermute x1, waiting for transfers between devices, extended_2(): lax.ppermute(head, axis, [((i + 1) % count, i) for i in range(ends)])  13.9 us
    dot_general x1, matrix products, body(): jnp.einsum('hqk,khd->qhd', weights, value_heads, preferred_element_type=j...  13.3 us
    unnamed x28, local copies, waits for them, and re-layouts  7.93 us
    all_to_all x1, starting transfers between devices, body(): lax.all_to_all(picked, ('bevy', 'bevx'), split_axis=0, concat_axis=0, til...  7.55 us
    all_to_all x1, waiting for transfers between devices, body(): lax.all_to_all(picked, ('bevy', 'bevx'), split_axis=0, concat_axis=0, til...  6.62 us
    dot_general x1, matrix products, body(): jnp.dot(attended, w_out, preferred_element_type=jnp.float32)  4.61 us
    all_gather x1, blocking collectives, body(): lax.all_gather(arrived_rows, 'cam', axis=0, tiled=True)  4.1 us
  transfers between devices with their start and end apart: 3, of which 2 were waited for; matrix products, arithmetic and copies ran while one was open for 6% of the time, Pallas kernels for 0%

commit v1 on v0

--- a/solution.py
+++ b/solution.py
@@ -1,6 +1,10 @@
+import functools
+
 import jax
 import jax.numpy as jnp
 from jax import lax
+from jax.experimental import pallas as pl
+from jax.experimental.pallas import tpu as pltpu
 from jax.sharding import PartitionSpec as P
 
 ROWS_DEV = 8
@@ -25,7 +29,7 @@
     return cells
 
 
-def body(
+def dense_body(
     image_tokens,
     lift_weight,
     route_token,
@@ -105,6 +109,268 @@
     return result.astype(jnp.bfloat16).reshape(ROWS_DEV, COLS_DEV, width_out)
 
 
+COL_TILE = 256
+NEVER = -1e30
+
+
+def to_column(row):
+    size = row.shape[1]
+    across = lax.broadcasted_iota(jnp.int32, (size, size), 1)
+    down = lax.broadcasted_iota(jnp.int32, (size, size), 0)
+    return jnp.sum(jnp.where(across == down, row, 0), axis=1, keepdims=True)
+
+
+def dot_last(left, right):
+    return lax.dot_general(
+        left, right, (((1,), (1,)), ((), ())), preferred_element_type=jnp.float32
+    )
+
+
+def slot_masks(cells, shift, exists, window):
+    size = cells.shape[1]
+    column = to_column(cells)
+    same = column == cells
+    down = lax.broadcasted_iota(jnp.int32, (size, size), 0)
+    across = lax.broadcasted_iota(jnp.int32, (size, size), 1)
+    repeat_row = jnp.sum(jnp.where(same & (down < across), 1, 0), axis=0, keepdims=True)
+    repeat_col = jnp.sum(jnp.where(same & (across < down), 1, 0), axis=1, keepdims=True)
+
+    def place(cell, repeat):
+        spot = cell + shift
+        keep = (repeat == 0) & (spot >= 0) & (spot < window) & exists
+        return jnp.where(keep, spot, -1)
+
+    return same.astype(jnp.bfloat16), place(cells, repeat_row), place(column, repeat_col)
+
+
+def slot_attention(
+    cam,
+    row_start,
+    grid_rows,
+    cells_own,
+    cells_side,
+    rows_ref,
+    bias_ref,
+    gain_ref,
+    lift_ref,
+    query_w,
+    key_w,
+    value_w,
+    out_w,
+    out_ref,
+    proj,
+    lifted,
+    normed,
+    queries,
+    keys,
+    values,
+    key_extra,
+    rest_top,
+    rest_sum,
+    attended,
+    wait_for,
+):
+    slots = cells_own.shape[1]
+    heads, window = bias_ref.shape
+    width = proj.shape[1]
+    head_size = width // heads
+    own_cells = ROWS_DEV * COLS_DEV
+    tile_rows = 2 * ROWS_DEV
+    halo_cells = HALO * COLS_DEV
+    side_shift = (tile_rows - HALO) * COLS_DEV
+    own_same, own_row, own_col = slot_masks(
+        cells_own, halo_cells - cam * own_cells, True, window
+    )
+    side_exists = jnp.where(cam == 0, row_start > 0, row_start + ROWS_DEV < grid_rows)
+    side_same, side_row, side_col = slot_masks(
+        cells_side, jnp.where(cam == 0, -side_shift, side_shift), side_exists, window
+    )
+    spot_row = jnp.concatenate([own_row, side_row], axis=1)
+    spot_col = jnp.concatenate([own_col, side_col], axis=0)
+    hit = lax.broadcasted_iota(jnp.int32, (2 * slots, window), 1) == spot_col
+    taken = jnp.max(jnp.where(hit, 1.0, 0.0), axis=0, keepdims=True) > 0.5
+    bias = bias_ref[...]
+    extra = dot_last(bias, hit.astype(jnp.bfloat16))
+    extra = jnp.where(spot_row >= 0, extra, NEVER)
+    key_extra[...] = extra
+    window_row = row_start - HALO + lax.broadcasted_iota(jnp.int32, (1, window), 1) // COLS_DEV
+    empty = jnp.logical_not(taken) & (window_row >= 0) & (window_row < grid_rows)
+    rest = jnp.where(empty, bias.astype(jnp.float32), NEVER)
+    top = jnp.max(rest, axis=1, keepdims=True)
+    total = jnp.sum(jnp.where(empty, jnp.exp(rest - top), 0.0), axis=1, keepdims=True)
+    rest_top[...] = jnp.broadcast_to(top, rest_top.shape)
+    rest_sum[...] = jnp.broadcast_to(total, rest_sum.shape)
+
+    wait_for("lift")
+
+    @pl.loop(0, width // COL_TILE)
+    def _(step):
+        cols = pl.ds(pl.multiple_of(step * COL_TILE, COL_TILE), COL_TILE)
+        proj[:, cols] = jnp.dot(
+            rows_ref[...], lift_ref[:, cols], preferred_element_type=jnp.float32
+        ).astype(jnp.bfloat16)
+        lifted[:slots, cols] = jnp.dot(
+            own_same, proj[:slots, cols], preferred_element_type=jnp.float32
+        )
+        lifted[slots:, cols] = jnp.dot(
+            side_same, proj[slots:, cols], preferred_element_type=jnp.float32
+        )
+
+    whole = lifted[...]
+    mean_square = jnp.mean(whole * whole, axis=-1, keepdims=True)
+    normed[...] = (whole * lax.rsqrt(mean_square + 1e-06) * gain_ref[...]).astype(jnp.bfloat16)
+
+    wait_for("qkv")
+
+    @pl.loop(0, width // COL_TILE)
+    def _(step):
+        cols = pl.ds(pl.multiple_of(step * COL_TILE, COL_TILE), COL_TILE)
+        made = jnp.dot(
+            normed[:slots, :], query_w[:, cols], preferred_element_type=jnp.float32
+        ).astype(jnp.bfloat16)
+        queries[:, cols] = made * jnp.asarray(head_size**-0.5, jnp.bfloat16)
+        keys[:, cols] = jnp.dot(
+            normed[...], key_w[:, cols], preferred_element_type=jnp.float32
+        ).astype(jnp.bfloat16)
+        values[:, cols] = jnp.dot(
+            normed[...], value_w[:, cols], preferred_element_type=jnp.float32
+        ).astype(jnp.bfloat16)
+
+    blank_top = jnp.maximum(jnp.max(extra, axis=1, keepdims=True), top)
+    blank = jnp.exp(extra - blank_top)
+    blank_sum = jnp.sum(blank, axis=1, keepdims=True) + total * jnp.exp(top - blank_top)
+    blank = (blank / blank_sum).astype(jnp.bfloat16)
+    blank = jnp.dot(blank, values[...], preferred_element_type=jnp.float32)
+    lane_head = lax.broadcasted_iota(jnp.int32, (heads, width), 1) // head_size
+    own_head = lax.broadcasted_iota(jnp.int32, (heads, width), 0) == lane_head
+    blank = jnp.sum(jnp.where(own_head, blank, 0.0), axis=0, keepdims=True)
+    attended[slots:, :] = jnp.broadcast_to(blank, (16, width)).astype(jnp.bfloat16)
+
+    low = lax.broadcasted_iota(jnp.int32, (slots, 2 * head_size), 1) < head_size
+
+    @pl.loop(0, heads // 4)
+    def _(step):
+        for inner in range(2):
+            pair = step * 2 + inner
+            cols = pl.ds(pl.multiple_of(pair * 2 * head_size, 2 * head_size), 2 * head_size)
+            query = queries[:, cols]
+            parts = []
+            for side in range(2):
+                head = pl.ds(pair * 2 + side, 1)
+                mine = low if side == 0 else jnp.logical_not(low)
+                score = dot_last(jnp.where(mine, query, jnp.zeros_like(query)), keys[:, cols])
+                score = score + key_extra[head, :]
+                rest_best = rest_top[head, :][:, :1]
+                best = jnp.maximum(jnp.max(score, axis=1, keepdims=True), rest_best)
+                expo = jnp.exp(score - best)
+                weight_sum = jnp.sum(expo, axis=1, keepdims=True)
+                weight_sum = weight_sum + rest_sum[head, :][:, :1] * jnp.exp(rest_best - best)
+                mixed = jnp.dot(
+                    expo.astype(jnp.bfloat16), values[:, cols], preferred_element_type=jnp.float32
+                )
+                parts.append(mixed / weight_sum)
+            attended[:slots, cols] = jnp.where(low, parts[0], parts[1]).astype(jnp.bfloat16)
+
+    cell = lax.broadcasted_iota(jnp.int32, (own_cells, slots), 0) + halo_cells
+    spread = cell == own_row
+    filled = jnp.max(jnp.where(spread, 1.0, 0.0), axis=1, keepdims=True) > 0.5
+    spread = spread.astype(jnp.bfloat16)
+
+    wait_for("out")
+
+    @pl.loop(0, width // COL_TILE)
+    def _(step):
+        cols = pl.ds(pl.multiple_of(step * COL_TILE, COL_TILE), COL_TILE)
+        mixed = jnp.dot(attended[...], out_w[:, cols], preferred_element_type=jnp.float32)
+        final = (lifted[:slots, cols] + mixed[:slots]).astype(jnp.bfloat16)
+        placed = jnp.dot(spread, final, preferred_element_type=jnp.float32)
+        out_ref[:, cols] = jnp.where(filled, placed, mixed[slots : slots + 1]).astype(jnp.bfloat16)
+
+
+def compute_scratch(slots, heads, width):
+    return [
+        pltpu.VMEM((2 * slots, width), jnp.bfloat16),
+        pltpu.VMEM((2 * slots, width), jnp.float32),
+        pltpu.VMEM((2 * slots, width), jnp.bfloat16),
+        pltpu.VMEM((slots, width), jnp.bfloat16),
+        pltpu.VMEM((2 * slots, width), jnp.bfloat16),
+        pltpu.VMEM((2 * slots, width), jnp.bfloat16),
+        pltpu.VMEM((heads, 2 * slots), jnp.float32),
+        pltpu.VMEM((heads, 128), jnp.float32),
+        pltpu.VMEM((heads, 128), jnp.float32),
+        pltpu.VMEM((slots + 16, width), jnp.bfloat16),
+    ]
+
+
+def compute_kernel(
+    grid_rows, cells_ref, rows_ref, bias_ref, gain_ref, lift_h, query_h, key_h, value_h, out_h,
+    out_ref, lift_v, query_v, key_v, value_v, out_v, sems, *scratch
+):
+    pairs = [(lift_h, lift_v), (query_h, query_v), (key_h, key_v), (value_h, value_v), (out_h, out_v)]
+    copies = [pltpu.make_async_copy(a, b, sems.at[i]) for i, (a, b) in enumerate(pairs)]
+    for copy in copies:
+        copy.start()
+
+    def wait_for(name):
+        for copy in {"lift": copies[:1], "qkv": copies[1:4], "out": copies[4:]}[name]:
+            copy.wait()
+
+    cam = lax.axis_index("cam")
+    row_start = (lax.axis_index("bevy") * 2 + cam) * ROWS_DEV
+    slot_attention(
+        cam, row_start, grid_rows, cells_ref[0:1, :], cells_ref[1:2, :], rows_ref, bias_ref,
+        gain_ref, lift_v, query_v, key_v, value_v, out_v, out_ref, *scratch, wait_for,
+    )
+
+
+def slot_body(
+    image_tokens, lift_weight, route_token, route_cell, slot_counts, norm_gain, w_query, w_key,
+    w_value, w_out, key_bias,
+):
+    tile_count, slot_count = route_token.shape[2:]
+    width = lift_weight.shape[1]
+    heads = key_bias.shape[2]
+    grid_rows = key_bias.shape[0]
+    live = lax.broadcasted_iota(jnp.int32, (tile_count, slot_count), 1) < slot_counts[0, 0][:, None]
+    wanted = jnp.where(live, route_token[0, 0], -1).reshape(-1, 1)
+    choose = (
+        lax.broadcasted_iota(jnp.int32, (1, image_tokens.shape[0]), 1) == wanted
+    ).astype(jnp.bfloat16)
+    picked = jnp.dot(choose, image_tokens, preferred_element_type=jnp.float32).astype(jnp.bfloat16)
+    picked = picked.reshape(tile_count, slot_count, -1)
+    arrived = lax.all_to_all(picked, ("bevy", "bevx"), split_axis=0, concat_axis=0, tiled=True)
+    arrived = arrived.reshape(tile_count * slot_count, -1)
+    cells = route_cell[:, 0, 0, :].reshape(-1)
+    swap = [(0, 1), (1, 0)]
+    edge = 2 * lax.axis_size("bevy")
+    across = [p for i in range(1, edge - 1, 2) for p in ((i, i + 1), (i + 1, i))]
+    own_cells = jnp.concatenate([cells, lax.ppermute(cells, "cam", swap)])
+    side_cells = lax.ppermute(own_cells, ("bevy", "cam"), across)
+    own_rows = jnp.concatenate([arrived, lax.ppermute(arrived, "cam", swap)])
+    side_rows = lax.ppermute(own_rows, ("bevy", "cam"), across)
+    rows = jnp.concatenate([own_rows, side_rows])
+    both_cells = jnp.stack([own_cells, side_cells])
+    row_start = lax.axis_index(("bevy", "cam")) * ROWS_DEV
+    padded = jnp.pad(key_bias, ((HALO, HALO), (0, 0), (0, 0)))
+    window = lax.dynamic_slice_in_dim(padded, row_start, 2 * ROWS_DEV, 0)
+    window = window.reshape(-1, heads).T
+    slots = 2 * tile_count * slot_count
+    vmem = pl.BlockSpec(memory_space=pltpu.VMEM)
+    anywhere = pl.BlockSpec(memory_space=pl.ANY)
+    weights = (lift_weight, w_query, w_key, w_value, w_out)
+    out = pl.pallas_call(
+        functools.partial(compute_kernel, grid_rows),
+        out_shape=jax.ShapeDtypeStruct((ROWS_DEV * COLS_DEV, width), jnp.bfloat16),
+        in_specs=[vmem] * 4 + [anywhere] * 5,
+        out_specs=vmem,
+        scratch_shapes=[pltpu.VMEM(w.shape, jnp.bfloat16) for w in weights]
+        + [pltpu.SemaphoreType.DMA((5,))]
+        + compute_scratch(slots, heads, width),
+        compiler_params=pltpu.CompilerParams(vmem_limit_bytes=48 * 2**20),
+    )(both_cells, rows, window, norm_gain.reshape(1, -1), *weights)
+    return out.reshape(ROWS_DEV, COLS_DEV, width)
+
+
 def solution(mesh):
     placed = (
         P(("bevy", "bevx", "cam"), None),
@@ -119,8 +385,10 @@
         P(),
         P(None, "bevx", None),
     )
+    tiles = mesh.shape["bevy"] * mesh.shape["bevx"]
+    sparse = mesh.shape["cam"] == 2 and tiles <= 16
     return jax.shard_map(
-        body,
+        slot_body if sparse else dense_body,
         mesh=mesh,
         in_specs=placed,
         out_specs=P(("bevy", "cam"), "bevx", None),

time: 106 us -> 55.4 us (0.52); the launches traced: 104 us -> 55.1 us
  matrix products: 43.9 us -> 0.25 us
  Pallas kernels: 0 us -> 19.1 us
  waiting for transfers between devices: 20.6 us -> 7.28 us
  local copies, waits for them, and re-layouts: 12.4 us -> 3.42 us
  blocking collectives: 6.52 us -> 14.1 us
  other arithmetic: 7.35 us -> 1.88 us
  starting transfers between devices: 13.3 us -> 8.97 us
    dot_general x7 -> x1, matrix products: 25.9 us -> 0.25 us  [slot_body(): jnp.dot(choose, image_tokens, preferred_element_type=jnp.float32)]
    pallas_call x0 -> x1, Pallas kernels: none -> 19.1 us  [slot_body(): pl.pallas_call(functools.partial(compute_kernel, grid_rows), out_shape=ja...]
    sub x1 -> x0, matrix products: 17.9 us -> none  [body(): expo = jnp.exp(scores - top_score)]
    all_to_all x0 -> x1, blocking collectives: none -> 14.1 us  [slot_body(): lax.all_to_all(picked, ('bevy', 'bevx'), split_axis=0, concat_axis=0, til...]
    all_to_all x1 -> x0, starting transfers between devices: 7.55 us -> none  [body(): lax.all_to_all(picked, ('bevy', 'bevx'), split_axis=0, concat_axis=0, til...]
    ppermute x2 -> x4, waiting for transfers between devices: 13.9 us -> 7.28 us  [the longest x1 7.27 us: slot_body(): side_cells = lax.ppermute(own_cells, ('bevy', 'cam'), across)]
    all_to_all x1 -> x0, waiting for transfers between devices: 6.62 us -> none  [body(): lax.all_to_all(picked, ('bevy', 'bevx'), split_axis=0, concat_axis=0, til...]
    all_gather x2 -> x0, blocking collectives: 6.52 us -> none  [the longest x1 4.1 us: body(): lax.all_gather(arrived_rows, 'cam', axis=0, tiled=True)]
  transfers between devices with their start and end apart: 3 -> 4, of which waited for: 2 -> 1; matrix products, arithmetic and copies ran while one was open for 6% -> 2% of each run, Pallas kernels for 0% -> 0%
where the time goes in v1:
time: 55.4 us; the launch traced here: 55.1 us
  Pallas kernels  19.1 us (34%)
  blocking collectives  14.1 us (25%)
  starting transfers between devices  8.97 us (16%)
  waiting for transfers between devices  7.28 us (13%)
  local copies, waits for them, and re-layouts  3.42 us (6%)
  other arithmetic  1.88 us (3%)
    pallas_call x1, Pallas kernels, slot_body(): pl.pallas_call(functools.partial(compute_kernel, grid_rows), out_shape=ja...  19.1 us
    all_to_all x1, blocking collectives, slot_body(): lax.all_to_all(picked, ('bevy', 'bevx'), split_axis=0, concat_axis=0, til...  14.1 us
    ppermute x1, waiting for transfers between devices, slot_body(): side_cells = lax.ppermute(own_cells, ('bevy', 'cam'), across)  7.27 us
    ppermute x1, starting transfers between devices, slot_body(): side_cells = lax.ppermute(own_cells, ('bevy', 'cam'), across)  3.64 us
    ppermute x1, starting transfers between devices, slot_body(): own_rows = jnp.concatenate([arrived, lax.ppermute(arrived, 'cam', swap)])  3.19 us
    unnamed x13, local copies, waits for them, and re-layouts  2.95 us
    ppermute x1, starting transfers between devices, slot_body(): side_rows = lax.ppermute(own_rows, ('bevy', 'cam'), across)  1.92 us
  transfers between devices with their start and end apart: 4, of which 1 were waited for; matrix products, arithmetic and copies ran while one was open for 2% of the time, Pallas kernels for 0%

profile of v1, /device:TPU:1, one launch (start us, length us, event | category | flops | bytes accessed | tf_op | source)
XLA Modules:
  0.0 55.1 jit_solution(8137997116486134615)
XLA Ops:
  0.0 0.0 copy-start
  0.0 0.8 %iota_compare_fusion.2 = pred[16,8]{1,0:T(8,128)(4,1)S(1)} fusion(s32[16]{0:T(128)} %bitcast.25), kind=kLoop, calls=%fused_computation.7 | loop fusion | flops 128 | bytes 192 | tf_op jit(solution)/shard_map/lt | solution.py:334
  0.8 0.1 lt.23
  0.9 0.8 %copy.16 = s32[1,1,16,8]{3,2,1,0:T(8,128)S(1)} copy(s32[1,1,16,8]{2,3,1,0:T(8,128)} %param.13) | data formatting | bytes 1024 | tf_op args[2]
  1.7 0.1 squeeze.3
  1.8 0.0 copy-done
  1.8 0.2 fusion
  2.0 14.1 %all_to_all.5 = bf16[16,8,768]{2,1,0:T(8,128)(2,1)S(1)} all-to-all(bf16[16,8,768]{2,1,0:T(8,128)(2,1)S(1)} %fusion), channel_id=1, replica_groups=mesh['bevy'=4,'bevx'=4,'cam'=2] {'bevy','bevx'}, dimensions={0} | all-to-all | bytes 393216 | tf_op jit(solution)/shard_map/all_to_all | solution.py:341
  16.2 3.2 %collective-permute-start.2 = (bf16[128,768]{1,0:T(8,128)(2,1)S(1)}, bf16[128,768]{1,0:T(8,128)(2,1)S(1)}, u32[]{:S(2)}, u32[]{:S(2)}) collective-permute-start(bf16[128,768]{1,0:T(8,128)(2,1)S(1)} %bitcast.20), channel_id=1, source_target_pairs={{0,1},{1,0},{2,3},{3,2},{4,5},{5,4},{6,7},{7,6},{8,9},{9,8},{10,11... | collective-permute-start | bytes 589832 | tf_op jit(solution)/shard_map/ppermute | solution.py:349
  19.4 0.8 %copy.15 = s32[16,1,1,8]{3,0,2,1:T(8,128)S(1)} copy(s32[16,1,1,8]{0,3,2,1:T(8,128)} %param.14) | data formatting | bytes 1024 | tf_op args[3]
  20.1 0.1 reshape_squeeze.3
  20.2 0.2 collective-permute-start
  20.4 0.0 collective-permute-done.2
  20.5 1.9 %collective-permute-start.3 = (bf16[256,768]{1,0:T(8,128)(2,1)S(1)}, bf16[256,768]{1,0:T(8,128)(2,1)}, u32[]{:S(2)}, u32[]{:S(2)}) collective-permute-start(bf16[256,768]{1,0:T(8,128)(2,1)S(1)} %pad_maximum_fusion.1), channel_id=1, source_target_pairs={{1,8},{8,1},{9,16},{16,9},{17,24},{24,17},{3,10},{10,3},{11,18},{1... | collective-permute-start | bytes 1179656 | tf_op jit(solution)/shard_map/ppermute | solution.py:350
  22.4 0.0 collective-permute-done
  22.4 3.6 %collective-permute-start.1 = (s32[256]{0:T(256)S(1)}, s32[256]{0:T(256)S(1)}, u32[]{:S(2)}, u32[]{:S(2)}) collective-permute-start(s32[256]{0:T(256)S(1)} %constant_dynamic-update-slice_fusion), channel_id=1, source_target_pairs={{1,8},{8,1},{9,16},{16,9},{17,24},{24,17},{3,10},{10,3},{11,18},{1... | collective-permute-start | bytes 3080 | tf_op jit(solution)/shard_map/ppermute | solution.py:348
  26.1 0.1 pad_dynamic-slice_fusion
  26.2 0.1 reshape.38
  26.3 7.3 %collective-permute-done.1 = s32[256]{0:T(256)S(1)} collective-permute-done((s32[256]{0:T(256)S(1)}, s32[256]{0:T(256)S(1)}, u32[]{:S(2)}, u32[]{:S(2)}) %collective-permute-start.1) | collective-permute-done | bytes 1056 | tf_op jit(solution)/shard_map/ppermute | solution.py:348
  33.6 0.0 collective-permute-done.3
  33.6 1.0 %pad_maximum_fusion.rows_ref = bf16[512,768]{1,0:T(8,128)(2,1)S(1)} fusion(bf16[256,768]{1,0:T(8,128)(2,1)} %collective-permute-done.3, bf16[128,768]{1,0:T(8,128)(2,1)S(1)} %collective-permute-done.2, bf16[128,768]{1,0:T(8,128)(2,1)S(1)} %bitcast.22), kind=kLoop, calls=%fused_computation.2 | loop fusion | flops 2359296 | bytes 1572864 | tf_op jit(solution)/shard_map/concatenate | solution.py:351
  34.7 0.0 copy-start.2
  34.7 1.4 %copy-done.2 = bf16[768,1024]{1,0:T(8,128)(2,1)S(1)} copy-done((bf16[768,1024]{1,0:T(8,128)(2,1)S(1)}, bf16[768,1024]{1,0:T(8,128)(2,1)}, u32[]{:S(2)}) %copy-start.2) | copy-done | bytes 1572888
  36.1 19.1 %shard_map.109 = bf16[512,1024]{1,0:T(8,128)(2,1)} custom-call(s32[2,256]{1,0:T(2,128)S(1)} %pad_add_fusion.cells_ref, bf16[512,768]{1,0:T(8,128)(2,1)S(1)} %pad_maximum_fusion.rows_ref, bf16[16,1024]{1,0:T(8,128)(2,1)S(1)} %bitcast.18, f32[1,1024]{1,0:T(1,128)S(1)} %bitcast.19, bf16[768,1024]{1,0:T(8,128)(2,1)S(1)} %copy-done.2, ...), custom_call_target="tpu_custom_call" | custom-call | tf_op jit(solution)/shard_map/pallas_call | solution.py:361
  (13 shorter events, 0.1 us)
Async XLA Ops:
  0.0 1.8 %copy-start = (bf16[256,768]{1,0:T(8,128)(2,1)S(1)}, bf16[256,768]{1,0:T(8,128)(2,1)}, u32[]{:S(2)}) copy-start(bf16[256,768]{1,0:T(8,128)(2,1)} %param.11) | copy-start | bytes 1179652
  0.0 26.1 %copy-start.4 = (bf16[64,64,16]{1,2,0:T(8,128)(2,1)S(1)}, bf16[64,64,16]{1,2,0:T(8,128)(2,1)}, u32[]{:S(2)}) copy-start(bf16[64,64,16]{1,2,0:T(8,128)(2,1)} %param.21) | copy-start | bytes 393220
  16.2 18.5 %copy-start.1 = (bf16[1024,1024]{1,0:T(8,128)(2,1)S(1)}, bf16[1024,1024]{1,0:T(8,128)(2,1)}, u32[]{:S(2)}) copy-start(bf16[1024,1024]{1,0:T(8,128)(2,1)} %query_h.1) | copy-start | bytes 6291460
  16.2 18.5 %copy-start.3 = (f32[1024]{0:T(1024)S(1)}, f32[1024]{0:T(1024)}, u32[]{:S(2)}) copy-start(f32[1024]{0:T(1024)} %param.16) | copy-start | bytes 12292
  16.2 4.3 %collective-permute-start.2 = (bf16[128,768]{1,0:T(8,128)(2,1)S(1)}, bf16[128,768]{1,0:T(8,128)(2,1)S(1)}, u32[]{:S(2)}, u32[]{:S(2)}) collective-permute-start(bf16[128,768]{1,0:T(8,128)(2,1)S(1)} %bitcast.20), channel_id=1, source_target_pairs={{0,1},{1,0},{2,3},{3,2},{4,5},{5,4},{6,7},{7,6},{8,9},{9,8},{10,11... | collective-permute-start | bytes 589832 | tf_op jit(solution)/shard_map/ppermute | solution.py:349
  20.2 2.2 %collective-permute-start = (s32[128]{0:T(128)S(1)}, s32[128]{0:T(128)S(1)}, u32[]{:S(2)}, u32[]{:S(2)}) collective-permute-start(s32[128]{0:T(128)S(1)} %reshape_squeeze.3), channel_id=1, source_target_pairs={{0,1},{1,0},{2,3},{3,2},{4,5},{5,4},{6,7},{7,6},{8,9},{9,8},{10,11... | collective-permute-start | bytes 1544 | tf_op jit(solution)/shard_map/ppermute | solution.py:347
  20.5 13.1 %collective-permute-start.3 = (bf16[256,768]{1,0:T(8,128)(2,1)S(1)}, bf16[256,768]{1,0:T(8,128)(2,1)}, u32[]{:S(2)}, u32[]{:S(2)}) collective-permute-start(bf16[256,768]{1,0:T(8,128)(2,1)S(1)} %pad_maximum_fusion.1), channel_id=1, source_target_pairs={{1,8},{8,1},{9,16},{16,9},{17,24},{24,17},{3,10},{10,3},{11,18},{1... | collective-permute-start | bytes 1179656 | tf_op jit(solution)/shard_map/ppermute | solution.py:350
  22.4 11.1 %collective-permute-start.1 = (s32[256]{0:T(256)S(1)}, s32[256]{0:T(256)S(1)}, u32[]{:S(2)}, u32[]{:S(2)}) collective-permute-start(s32[256]{0:T(256)S(1)} %constant_dynamic-update-slice_fusion), channel_id=1, source_target_pairs={{1,8},{8,1},{9,16},{16,9},{17,24},{24,17},{3,10},{10,3},{11,18},{1... | collective-permute-start | bytes 3080 | tf_op jit(solution)/shard_map/ppermute | solution.py:348
  34.7 1.4 %copy-start.2 = (bf16[768,1024]{1,0:T(8,128)(2,1)S(1)}, bf16[768,1024]{1,0:T(8,128)(2,1)}, u32[]{:S(2)}) copy-start(bf16[768,1024]{1,0:T(8,128)(2,1)} %lift_h.1) | copy-start | bytes 4718596

commit v2 on v1

--- a/solution.py
+++ b/solution.py
@@ -111,6 +111,7 @@
 
 COL_TILE = 256
 NEVER = -1e30
+SLOTS = 8
 
 
 def to_column(row):
@@ -158,7 +159,6 @@
     value_w,
     out_w,
     out_ref,
-    proj,
     lifted,
     normed,
     queries,
@@ -172,7 +172,7 @@
 ):
     slots = cells_own.shape[1]
     heads, window = bias_ref.shape
-    width = proj.shape[1]
+    width = lifted.shape[1]
     head_size = width // heads
     own_cells = ROWS_DEV * COLS_DEV
     tile_rows = 2 * ROWS_DEV
@@ -201,40 +201,49 @@
     rest_top[...] = jnp.broadcast_to(top, rest_top.shape)
     rest_sum[...] = jnp.broadcast_to(total, rest_sum.shape)
 
+    def lift_group(group, same):
+        part = pl.ds(group * slots, slots)
+
+        @pl.loop(0, width // COL_TILE)
+        def _(step):
+            cols = pl.ds(pl.multiple_of(step * COL_TILE, COL_TILE), COL_TILE)
+            made = jnp.dot(rows_ref[part, :], lift_ref[:, cols], preferred_element_type=jnp.float32)
+            lifted[part, cols] = jnp.dot(
+                same, made.astype(jnp.bfloat16), preferred_element_type=jnp.float32
+            )
+
+        whole = lifted[part, :]
+        mean_square = jnp.mean(whole * whole, axis=-1, keepdims=True)
+        normed[part, :] = (whole * lax.rsqrt(mean_square + 1e-06) * gain_ref[...]).astype(
+            jnp.bfloat16
+        )
+
+    def key_group(group):
+        part = pl.ds(group * slots, slots)
+
+        @pl.loop(0, width // COL_TILE)
+        def _(step):
+            cols = pl.ds(pl.multiple_of(step * COL_TILE, COL_TILE), COL_TILE)
+            if group == 0:
+                made = jnp.dot(
+                    normed[part, :], query_w[:, cols], preferred_element_type=jnp.float32
+                ).astype(jnp.bfloat16)
+                queries[:, cols] = made * jnp.asarray(head_size**-0.5, jnp.bfloat16)
+            keys[part, cols] = jnp.dot(
+                normed[part, :], key_w[:, cols], preferred_element_type=jnp.float32
+            ).astype(jnp.bfloat16)
+            values[part, cols] = jnp.dot(
+                normed[part, :], value_w[:, cols], preferred_element_type=jnp.float32
+            ).astype(jnp.bfloat16)
+
+    wait_for("own")
     wait_for("lift")
-
-    @pl.loop(0, width // COL_TILE)
-    def _(step):
-        cols = pl.ds(pl.multiple_of(step * COL_TILE, COL_TILE), COL_TILE)
-        proj[:, cols] = jnp.dot(
-            rows_ref[...], lift_ref[:, cols], preferred_element_type=jnp.float32
-        ).astype(jnp.bfloat16)
-        lifted[:slots, cols] = jnp.dot(
-            own_same, proj[:slots, cols], preferred_element_type=jnp.float32
-        )
-        lifted[slots:, cols] = jnp.dot(
-            side_same, proj[slots:, cols], preferred_element_type=jnp.float32
-        )
-
-    whole = lifted[...]
-    mean_square = jnp.mean(whole * whole, axis=-1, keepdims=True)
-    normed[...] = (whole * lax.rsqrt(mean_square + 1e-06) * gain_ref[...]).astype(jnp.bfloat16)
-
+    lift_group(0, own_same)
     wait_for("qkv")
-
-    @pl.loop(0, width // COL_TILE)
-    def _(step):
-        cols = pl.ds(pl.multiple_of(step * COL_TILE, COL_TILE), COL_TILE)
-        made = jnp.dot(
-            normed[:slots, :], query_w[:, cols], preferred_element_type=jnp.float32
-        ).astype(jnp.bfloat16)
-        queries[:, cols] = made * jnp.asarray(head_size**-0.5, jnp.bfloat16)
-        keys[:, cols] = jnp.dot(
-            normed[...], key_w[:, cols], preferred_element_type=jnp.float32
-        ).astype(jnp.bfloat16)
-        values[:, cols] = jnp.dot(
-            normed[...], value_w[:, cols], preferred_element_type=jnp.float32
-        ).astype(jnp.bfloat16)
+    key_group(0)
+    wait_for("side")
+    lift_group(1, side_same)
+    key_group(1)
 
     blank_top = jnp.maximum(jnp.max(extra, axis=1, keepdims=True), top)
     blank = jnp.exp(extra - blank_top)
@@ -289,7 +298,6 @@
 
 def compute_scratch(slots, heads, width):
     return [
-        pltpu.VMEM((2 * slots, width), jnp.bfloat16),
         pltpu.VMEM((2 * slots, width), jnp.float32),
         pltpu.VMEM((2 * slots, width), jnp.bfloat16),
         pltpu.VMEM((slots, width), jnp.bfloat16),
@@ -302,25 +310,227 @@
     ]
 
 
-def compute_kernel(
-    grid_rows, cells_ref, rows_ref, bias_ref, gain_ref, lift_h, query_h, key_h, value_h, out_h,
-    out_ref, lift_v, query_v, key_v, value_v, out_v, sems, *scratch
+def fused_kernel(
+    grid_rows, wanted_ref, cells_ref, tokens_ref, bias_ref, gain_ref, lift_h, query_h, key_h,
+    value_h, out_h, out_ref, lift_v, query_v, key_v, value_v, out_v, weight_sems, sent, landed,
+    cells, rows, local_sem, tile_send, tile_recv, core_send, core_recv, side_send, side_recv,
+    cell_send, cell_recv, *scratch
 ):
+    bevy, bevx, cam = (lax.axis_index(name) for name in ("bevy", "bevx", "cam"))
+    count_y, count_x = lax.axis_size("bevy"), lax.axis_size("bevx")
+    tiles = count_y * count_x
+    me = bevy * count_x + bevx
+    block = 2 * SLOTS
+    group = count_x * block
+    half = sent.shape[1]
+    mesh_id = pl.DeviceIdType.MESH
+    has_up = bevy > 0
+    has_down = bevy < count_y - 1
+    has_side = jnp.where(cam == 0, bevy, count_y - 1 - bevy) > 0
+    mate = (bevy, bevx, 1 - cam)
+    up = (bevy - 1, bevx, 1)
+    down = (bevy + 1, bevx, 0)
+    across = (bevy + 2 * cam - 1, bevx, 1 - cam)
+
+    barrier = pltpu.get_barrier_semaphore()
+
+    @pl.loop(1, tiles)
+    def _(step):
+        peer = (me + step) % tiles
+        pl.semaphore_signal(
+            barrier, inc=1, device_id=(peer // count_x, peer % count_x, cam), device_id_type=mesh_id
+        )
+
+    pl.semaphore_signal(barrier, inc=1, device_id=mate, device_id_type=mesh_id)
+
+    @pl.when(has_side)
+    def _():
+        pl.semaphore_signal(barrier, inc=1, device_id=across, device_id_type=mesh_id)
+
+    wanted = to_column(wanted_ref[...])
+    choose = lax.broadcasted_iota(jnp.int32, (wanted.shape[0], tokens_ref.shape[0]), 1) == wanted
+    choose = choose.astype(jnp.bfloat16)
+    left = jnp.dot(choose, tokens_ref[:, :half], preferred_element_type=jnp.float32)
+    right = jnp.dot(choose, tokens_ref[:, half:], preferred_element_type=jnp.float32)
+    in_block = lax.broadcasted_iota(jnp.int32, left.shape, 0) % block
+    sent[...] = jnp.where(in_block < SLOTS, left, right).astype(jnp.bfloat16)
+
+    pl.semaphore_wait(barrier, tiles + jnp.where(has_side, 1, 0))
+
+    def at(start, size):
+        return pl.ds(pl.multiple_of(start, block), size)
+
+    def tile_copy(peer, slot):
+        return pltpu.make_async_remote_copy(
+            src_ref=sent.at[at(peer * block, block)],
+            dst_ref=landed.at[cam, at(slot * block, block)],
+            send_sem=tile_send.at[peer],
+            recv_sem=tile_recv.at[slot],
+            device_id=(peer // count_x, peer % count_x, cam),
+            device_id_type=mesh_id,
+        )
+
+    @pl.loop(1, tiles)
+    def _(step):
+        tile_copy((me + step) % tiles, me).start()
+
+    kept = pltpu.make_async_copy(
+        sent.at[at(me * block, block)], landed.at[cam, at(me * block, block)], local_sem.at[0]
+    )
+    kept.start()
+    own_cells = pltpu.make_async_copy(cells_ref, cells.at[cam], local_sem.at[1])
+    own_cells.start()
+
+    def cell_copy(target, slot, index, source):
+        return pltpu.make_async_remote_copy(
+            src_ref=cells_ref,
+            dst_ref=cells.at[slot],
+            send_sem=cell_send.at[index],
+            recv_sem=cell_recv.at[slot],
+            device_id=target,
+            device_id_type=mesh_id,
+        )
+
+    def row_copy(target, slot, part, send, recv):
+        return pltpu.make_async_remote_copy(
+            src_ref=landed.at[cam, at(part * group, group)],
+            dst_ref=landed.at[slot, at(part * group, group)],
+            send_sem=send,
+            recv_sem=recv,
+            device_id=target,
+            device_id_type=mesh_id,
+        )
+
+    def mate_rows(part, slot):
+        return row_copy(mate, slot, part, core_send.at[part], core_recv.at[part])
+
+    def side_rows(target, which, part, source):
+        return row_copy(
+            target, 2 + source, part, side_send.at[which, part], side_recv.at[source, part]
+        )
+
+    cell_copy(mate, cam, 0, cam).start()
+
+    @pl.when(has_up)
+    def _():
+        cell_copy(up, 2 + cam, 1, cam).start()
+
+    @pl.when(has_down)
+    def _():
+        cell_copy(down, 2 + cam, 2, cam).start()
+
     pairs = [(lift_h, lift_v), (query_h, query_v), (key_h, key_v), (value_h, value_v), (out_h, out_v)]
-    copies = [pltpu.make_async_copy(a, b, sems.at[i]) for i, (a, b) in enumerate(pairs)]
+    copies = [pltpu.make_async_copy(a, b, weight_sems.at[i]) for i, (a, b) in enumerate(pairs)]
     for copy in copies:
         copy.start()
 
+    kept.wait()
+
+    @pl.loop(0, count_y)
+    def _(step):
+        part = (bevy + step) % count_y
+
+        @pl.loop(0, count_x)
+        def _(index):
+            source = part * count_x + index
+
+            @pl.when(source != me)
+            def _():
+                tile_copy(source, source).wait_recv()
+
+        mate_rows(part, cam).start()
+
+        @pl.when(has_up)
+        def _():
+            side_rows(up, 0, part, cam).start()
+
+        @pl.when(has_down)
+        def _():
+            side_rows(down, 1, part, cam).start()
+
+    own_cells.wait()
+    cell_copy(mate, 1 - cam, 0, cam).wait_recv()
+
+    @pl.when(has_side)
+    def _():
+        cell_copy(across, 2, 0, cam).wait_recv()
+        cell_copy(across, 3, 0, cam).wait_recv()
+
+    @pl.when(jnp.logical_not(has_side))
+    def _():
+        cells[2:] = jnp.zeros_like(cells[2:])
+        landed[2:] = jnp.zeros_like(landed[2:])
+
+    slots = rows.shape[0] // 4
+
+    def join_halves(index):
+        slot = lax.broadcasted_iota(jnp.int32, (slots, landed.shape[1]), 0)
+        row = lax.broadcasted_iota(jnp.int32, (slots, landed.shape[1]), 1)
+        first = slot // SLOTS * block + slot % SLOTS
+        for side in range(2):
+            take = (row == first + side * SLOTS).astype(jnp.bfloat16)
+            rows[index * slots : (index + 1) * slots, side * half : (side + 1) * half] = jnp.dot(
+                take, landed[index], preferred_element_type=jnp.float32
+            ).astype(jnp.bfloat16)
+
     def wait_for(name):
+        if name == "own":
+
+            @pl.loop(0, count_y)
+            def _(part):
+                mate_rows(part, 1 - cam).wait_recv()
+
+            join_halves(0)
+            join_halves(1)
+            return
+        if name == "side":
+
+            @pl.when(has_side)
+            def _():
+                @pl.loop(0, count_y)
+                def _(part):
+                    side_rows(across, 0, part, 0).wait_recv()
+                    side_rows(across, 0, part, 1).wait_recv()
+
+            join_halves(2)
+            join_halves(3)
+            return
         for copy in {"lift": copies[:1], "qkv": copies[1:4], "out": copies[4:]}[name]:
             copy.wait()
 
-    cam = lax.axis_index("cam")
-    row_start = (lax.axis_index("bevy") * 2 + cam) * ROWS_DEV
+    row_start = (bevy * 2 + cam) * ROWS_DEV
+    cells_own = jnp.concatenate([cells[0, 0:1, :], cells[1, 0:1, :]], axis=1)
+    cells_side = jnp.concatenate([cells[2, 0:1, :], cells[3, 0:1, :]], axis=1)
     slot_attention(
-        cam, row_start, grid_rows, cells_ref[0:1, :], cells_ref[1:2, :], rows_ref, bias_ref,
-        gain_ref, lift_v, query_v, key_v, value_v, out_v, out_ref, *scratch, wait_for,
-    )
+        cam, row_start, grid_rows, cells_own, cells_side, rows, bias_ref, gain_ref, lift_v, query_v,
+        key_v, value_v, out_v, out_ref, *scratch, wait_for,
+    )
+
+    @pl.loop(1, tiles)
+    def _(step):
+        tile_copy((me + step) % tiles, me).wait_send()
+
+    @pl.loop(0, count_y)
+    def _(part):
+        mate_rows(part, cam).wait_send()
+
+    cell_copy(mate, cam, 0, cam).wait_send()
+
+    @pl.when(has_up)
+    def _():
+        cell_copy(up, 2 + cam, 1, cam).wait_send()
+
+        @pl.loop(0, count_y)
+        def _(part):
+            side_rows(up, 0, part, cam).wait_send()
+
+    @pl.when(has_down)
+    def _():
+        cell_copy(down, 2 + cam, 2, cam).wait_send()
+
+        @pl.loop(0, count_y)
+        def _(part):
+            side_rows(down, 1, part, cam).wait_send()
 
 
 def slot_body(
@@ -331,25 +541,11 @@
     width = lift_weight.shape[1]
     heads = key_bias.shape[2]
     grid_rows = key_bias.shape[0]
+    half = image_tokens.shape[1] // 2
     live = lax.broadcasted_iota(jnp.int32, (tile_count, slot_count), 1) < slot_counts[0, 0][:, None]
-    wanted = jnp.where(live, route_token[0, 0], -1).reshape(-1, 1)
-    choose = (
-        lax.broadcasted_iota(jnp.int32, (1, image_tokens.shape[0]), 1) == wanted
-    ).astype(jnp.bfloat16)
-    picked = jnp.dot(choose, image_tokens, preferred_element_type=jnp.float32).astype(jnp.bfloat16)
-    picked = picked.reshape(tile_count, slot_count, -1)
-    arrived = lax.all_to_all(picked, ("bevy", "bevx"), split_axis=0, concat_axis=0, tiled=True)
-    arrived = arrived.reshape(tile_count * slot_count, -1)
-    cells = route_cell[:, 0, 0, :].reshape(-1)
-    swap = [(0, 1), (1, 0)]
-    edge = 2 * lax.axis_size("bevy")
-    across = [p for i in range(1, edge - 1, 2) for p in ((i, i + 1), (i + 1, i))]
-    own_cells = jnp.concatenate([cells, lax.ppermute(cells, "cam", swap)])
-    side_cells = lax.ppermute(own_cells, ("bevy", "cam"), across)
-    own_rows = jnp.concatenate([arrived, lax.ppermute(arrived, "cam", swap)])
-    side_rows = lax.ppermute(own_rows, ("bevy", "cam"), across)
-    rows = jnp.concatenate([own_rows, side_rows])
-    both_cells = jnp.stack([own_cells, side_cells])
+    wanted = jnp.where(live, route_token[0, 0], -1)[:, None, :]
+    wanted = jnp.broadcast_to(wanted, (tile_count, 2, slot_count)).reshape(1, -1)
+    cells = jnp.broadcast_to(route_cell.reshape(1, -1), (8, tile_count * slot_count))
     row_start = lax.axis_index(("bevy", "cam")) * ROWS_DEV
     padded = jnp.pad(key_bias, ((HALO, HALO), (0, 0), (0, 0)))
     window = lax.dynamic_slice_in_dim(padded, row_start, 2 * ROWS_DEV, 0)
@@ -358,16 +554,35 @@
     vmem = pl.BlockSpec(memory_space=pltpu.VMEM)
     anywhere = pl.BlockSpec(memory_space=pl.ANY)
     weights = (lift_weight, w_query, w_key, w_value, w_out)
+    count_y = lax.axis_size("bevy")
+    dma = pltpu.SemaphoreType.DMA
     out = pl.pallas_call(
-        functools.partial(compute_kernel, grid_rows),
+        functools.partial(fused_kernel, grid_rows),
         out_shape=jax.ShapeDtypeStruct((ROWS_DEV * COLS_DEV, width), jnp.bfloat16),
-        in_specs=[vmem] * 4 + [anywhere] * 5,
+        in_specs=[vmem] * 5 + [anywhere] * 5,
         out_specs=vmem,
         scratch_shapes=[pltpu.VMEM(w.shape, jnp.bfloat16) for w in weights]
-        + [pltpu.SemaphoreType.DMA((5,))]
+        + [
+            dma((5,)),
+            pltpu.VMEM((slots, half), jnp.bfloat16),
+            pltpu.VMEM((4, slots, half), jnp.bfloat16),
+            pltpu.VMEM((4,) + cells.shape, jnp.int32),
+            pltpu.VMEM((2 * slots, 2 * half), jnp.bfloat16),
+            dma((2,)),
+            dma((tile_count,)),
+            dma((tile_count,)),
+            dma((count_y,)),
+            dma((count_y,)),
+            dma((2, count_y)),
+            dma((2, count_y)),
+            dma((3,)),
+            dma((4,)),
+        ]
         + compute_scratch(slots, heads, width),
-        compiler_params=pltpu.CompilerParams(vmem_limit_bytes=48 * 2**20),
-    )(both_cells, rows, window, norm_gain.reshape(1, -1), *weights)
+        compiler_params=pltpu.CompilerParams(
+            vmem_limit_bytes=48 * 2**20, collective_id=0, has_side_effects=True
+        ),
+    )(wanted, cells, image_tokens, window, norm_gain.reshape(1, -1), *weights)
     return out.reshape(ROWS_DEV, COLS_DEV, width)
 
 

time: 55.4 us -> 43.9 us (0.79)
  Pallas kernels: 19.1 us -> 35.1 us
  blocking collectives: 14.1 us -> 0 us
  starting transfers between devices: 8.97 us -> 0 us
  waiting for transfers between devices: 7.28 us -> 0 us
  local copies, waits for them, and re-layouts: 3.42 us -> 7.68 us
  other arithmetic: 1.88 us -> 0.69 us
    pallas_call x1, Pallas kernels: 19.1 us -> 35.1 us  [slot_body(): pl.pallas_call(functools.partial(fused_kernel, grid_rows), out_shape=jax....]
    all_to_all x1 -> x0, blocking collectives: 14.1 us -> none  [slot_body(): lax.all_to_all(picked, ('bevy', 'bevx'), split_axis=0, concat_axis=0, til...]
    ppermute x4 -> x0, starting transfers between devices: 8.97 us -> none  [the longest x1 3.64 us: slot_body(): side_cells = lax.ppermute(own_cells, ('bevy', 'cam'), across)]
    ppermute x4 -> x0, waiting for transfers between devices: 7.28 us -> none  [the longest x1 7.27 us: slot_body(): side_cells = lax.ppermute(own_cells, ('bevy', 'cam'), across)]
    unnamed x13 -> x10, local copies, waits for them, and re-layouts: 2.95 us -> 6.41 us
    concatenate x2 -> x0, other arithmetic: 1.08 us -> none  [the longest x1 1.05 us: slot_body(): rows = jnp.concatenate([own_rows, side_rows])]
    dynamic_slice x2, local copies, waits for them, and re-layouts: 0.07 us -> 0.89 us  [slot_body(): window = lax.dynamic_slice_in_dim(padded, row_start, 2 * ROWS_DEV, 0)]
    lt x1 -> x0, other arithmetic: 0.79 us -> none  [slot_body(): lax.broadcasted_iota(jnp.int32, (tile_count, slot_count), 1)]
  transfers between devices with their start and end apart: 4 -> 0, of which waited for: 1 -> 0; matrix products, arithmetic and copies ran while one was open for 2% -> 0% of each run, Pallas kernels for 0% -> 0%
where the time goes in v2:
time: 43.9 us; the launch traced here: 43.5 us
  Pallas kernels  35.1 us (80%)
  local copies, waits for them, and re-layouts  7.68 us (17%)
  other arithmetic  0.69 us (2%)
    pallas_call x1, Pallas kernels, slot_body(): pl.pallas_call(functools.partial(fused_kernel, grid_rows), out_shape=jax....  35.1 us
    unnamed x10, local copies, waits for them, and re-layouts  6.41 us
    dynamic_slice x2, local copies, waits for them, and re-layouts, slot_body(): window = lax.dynamic_slice_in_dim(padded, row_start, 2 * ROWS_DEV, 0)  0.89 us

profile of v2, /device:TPU:1, one launch (start us, length us, event | category | flops | bytes accessed | tf_op | source)
XLA Modules:
  0.0 43.5 jit_solution(17595185452896933606)
XLA Ops:
  0.0 0.7 %bitcast_select_fusion = s32[16,8]{0,1:T(8,128)S(1)} fusion(s32[1,1,16,8]{2,3,1,0:T(8,128)} %param.13, s32[16]{0:T(128)} %bitcast.15), kind=kLoop, calls=%fused_computation.1 | loop fusion | flops 256 | bytes 1088 | tf_op jit(solution)/shard_map/jit(_where)/select_n | solution.py:546
  0.7 0.1 copy.15
  0.8 0.1 reshape.37.wanted_ref
  0.9 0.8 %copy.16 = s32[16,1,1,8]{3,0,2,1:T(8,128)S(1)} copy(s32[16,1,1,8]{0,3,2,1:T(8,128)} %param.14) | data formatting | bytes 1024 | tf_op args[3]
  1.6 0.1 broadcast_in_dim.19
  1.7 0.9 %pad_dynamic-slice_fusion = bf16[16,64,16]{1,2,0:T(8,128)(2,1)S(1)} fusion(s32[]{:T(128)S(6)} %select_n.12, bf16[64,64,16]{1,2,0:T(8,128)(2,1)} %param.21), kind=kLoop, calls=%fused_computation | loop fusion | bytes 163844 | tf_op jit(solution)/shard_map/dynamic_slice | solution.py:551
  2.6 0.1 reshape.38
  2.8 0.0 copy-start
  2.8 1.6 %copy-done = bf16[1024,1024]{1,0:T(8,128)(2,1)S(1)} copy-done((bf16[1024,1024]{1,0:T(8,128)(2,1)S(1)}, bf16[1024,1024]{1,0:T(8,128)(2,1)}, u32[]{:S(2)}) %copy-start) | copy-done | bytes 2097176
  4.3 0.0 copy-start.1
  4.3 1.4 %copy-done.1 = bf16[768,1024]{1,0:T(8,128)(2,1)S(1)} copy-done((bf16[768,1024]{1,0:T(8,128)(2,1)S(1)}, bf16[768,1024]{1,0:T(8,128)(2,1)}, u32[]{:S(2)}) %copy-start.1) | copy-done | bytes 1572888
  5.8 0.0 copy-start.2
  5.8 1.0 %copy-done.2 = bf16[256,768]{1,0:T(8,128)(2,1)S(1)} copy-done((bf16[256,768]{1,0:T(8,128)(2,1)S(1)}, bf16[256,768]{1,0:T(8,128)(2,1)}, u32[]{:S(2)}) %copy-start.2) | copy-done | bytes 393240
  6.7 0.0 copy-start.3
  6.8 0.7 %copy-done.3 = f32[1024]{0:T(1024)S(1)} copy-done((f32[1024]{0:T(1024)S(1)}, f32[1024]{0:T(1024)}, u32[]{:S(2)}) %copy-start.3) | copy-done | bytes 4120
  7.4 35.1 %shard_map.109 = bf16[512,1024]{1,0:T(8,128)(2,1)S(1)} custom-call(s32[1,256]{1,0:T(1,128)S(1)} %reshape.37.wanted_ref, s32[8,128]{1,0:T(8,128)S(1)} %broadcast_in_dim.20.cells_ref, bf16[256,768]{1,0:T(8,128)(2,1)S(1)} %copy-done.2, bf16[16,1024]{1,0:T(8,128)(2,1)S(1)} %bitcast.13, f32[1,1024]{1,0:T(1,128)S(1)} %bitcast.14, bf16[768,1024]{1,0:T(8,128)(2,1)S(1)} %copy-done.1, ...), custom_call_target="tpu_custom_call" | custom-call | tf_op jit(solution)/shard_map/pallas_call | solution.py:559
  42.6 1.0 %copy.19 = bf16[8,64,1024]{2,1,0:T(8,128)(2,1)} copy(bf16[8,64,1024]{2,1,0:T(8,128)(2,1)S(1)} %bitcast.12) | data formatting | bytes 2097152
  (3 shorter events, 0.0 us)
Async XLA Ops:
  2.8 1.6 %copy-start = (bf16[1024,1024]{1,0:T(8,128)(2,1)S(1)}, bf16[1024,1024]{1,0:T(8,128)(2,1)}, u32[]{:S(2)}) copy-start(bf16[1024,1024]{1,0:T(8,128)(2,1)} %query_h.1) | copy-start | bytes 6291460
  4.3 1.4 %copy-start.1 = (bf16[768,1024]{1,0:T(8,128)(2,1)S(1)}, bf16[768,1024]{1,0:T(8,128)(2,1)}, u32[]{:S(2)}) copy-start(bf16[768,1024]{1,0:T(8,128)(2,1)} %lift_h.1) | copy-start | bytes 4718596
  5.8 1.0 %copy-start.2 = (bf16[256,768]{1,0:T(8,128)(2,1)S(1)}, bf16[256,768]{1,0:T(8,128)(2,1)}, u32[]{:S(2)}) copy-start(bf16[256,768]{1,0:T(8,128)(2,1)} %tokens_ref.1) | copy-start | bytes 1179652
  6.7 0.7 %copy-start.3 = (f32[1024]{0:T(1024)S(1)}, f32[1024]{0:T(1024)}, u32[]{:S(2)}) copy-start(f32[1024]{0:T(1024)} %param.16) | copy-start | bytes 12292

commit v3 on v2

--- a/solution.py
+++ b/solution.py
@@ -311,9 +311,9 @@
 
 
 def fused_kernel(
-    grid_rows, wanted_ref, cells_ref, tokens_ref, bias_ref, gain_ref, lift_h, query_h, key_h,
+    grid_rows, token_ref, cell_ref, count_ref, gain_ref, tokens_h, bias_h, lift_h, query_h, key_h,
     value_h, out_h, out_ref, lift_v, query_v, key_v, value_v, out_v, weight_sems, sent, landed,
-    cells, rows, local_sem, tile_send, tile_recv, core_send, core_recv, side_send, side_recv,
+    cells, rows, tokens_ref, bias_rows, cells_ref, bias_ref, local_sem, tile_send, tile_recv, core_send, core_recv, side_send, side_recv,
     cell_send, cell_recv, *scratch
 ):
     bevy, bevx, cam = (lax.axis_index(name) for name in ("bevy", "bevx", "cam"))
@@ -332,6 +332,21 @@
     down = (bevy + 1, bevx, 0)
     across = (bevy + 2 * cam - 1, bevx, 1 - cam)
 
+    row_start = (bevy * 2 + cam) * ROWS_DEV
+    tokens_in = pltpu.make_async_copy(tokens_h, tokens_ref, local_sem.at[2])
+    tokens_in.start()
+    above = jnp.maximum(row_start - HALO, 0)
+    below = jnp.minimum(row_start + ROWS_DEV, grid_rows - HALO)
+    ranges = [(above, 0, HALO), (row_start, HALO, ROWS_DEV), (below, HALO + ROWS_DEV, HALO)]
+    bias_in = [
+        pltpu.make_async_copy(
+            bias_h.at[pl.ds(first, size)], bias_rows.at[pl.ds(to, size)], local_sem.at[3 + i]
+        )
+        for i, (first, to, size) in enumerate(ranges)
+    ]
+    for copy in bias_in:
+        copy.start()
+
     barrier = pltpu.get_barrier_semaphore()
 
     @pl.loop(1, tiles)
@@ -347,7 +362,26 @@
     def _():
         pl.semaphore_signal(barrier, inc=1, device_id=across, device_id_type=mesh_id)
 
-    wanted = to_column(wanted_ref[...])
+    live = lax.broadcasted_iota(jnp.int32, token_ref.shape, 0) < count_ref[...]
+    wanted = jnp.where(live, token_ref[...], -1).astype(jnp.bfloat16)
+    line = lax.broadcasted_iota(jnp.int32, (sent.shape[0], tiles), 0)
+    at_tile = (lax.broadcasted_iota(jnp.int32, line.shape, 1) == line // block).astype(jnp.bfloat16)
+    wanted = dot_last(at_tile, wanted)
+    line = lax.broadcasted_iota(jnp.int32, wanted.shape, 0)
+    at_slot = lax.broadcasted_iota(jnp.int32, wanted.shape, 1) == line % SLOTS
+    wanted = jnp.sum(jnp.where(at_slot, wanted, 0.0), axis=1, keepdims=True).astype(jnp.int32)
+    lane = lax.broadcasted_iota(jnp.int32, (tiles, tiles * SLOTS), 1)
+    at_tile = lane // SLOTS == lax.broadcasted_iota(jnp.int32, lane.shape, 0)
+    at_tile = at_tile.astype(jnp.bfloat16)
+    high = (cell_ref[...] // 32).astype(jnp.bfloat16)
+    low = (cell_ref[...] % 32).astype(jnp.bfloat16)
+    high = jnp.dot(high, at_tile, preferred_element_type=jnp.float32)
+    low = jnp.dot(low, at_tile, preferred_element_type=jnp.float32)
+    lane = lax.broadcasted_iota(jnp.int32, high.shape, 1)
+    at_slot = lane % SLOTS == lax.broadcasted_iota(jnp.int32, high.shape, 0)
+    line = jnp.sum(jnp.where(at_slot, high * 32.0 + low, 0.0), axis=0, keepdims=True)
+    cells_ref[...] = jnp.broadcast_to(line.astype(jnp.int32), cells_ref.shape)
+    tokens_in.wait()
     choose = lax.broadcasted_iota(jnp.int32, (wanted.shape[0], tokens_ref.shape[0]), 1) == wanted
     choose = choose.astype(jnp.bfloat16)
     left = jnp.dot(choose, tokens_ref[:, :half], preferred_element_type=jnp.float32)
@@ -424,30 +458,9 @@
     for copy in copies:
         copy.start()
 
-    kept.wait()
-
-    @pl.loop(0, count_y)
-    def _(step):
-        part = (bevy + step) % count_y
-
-        @pl.loop(0, count_x)
-        def _(index):
-            source = part * count_x + index
-
-            @pl.when(source != me)
-            def _():
-                tile_copy(source, source).wait_recv()
-
-        mate_rows(part, cam).start()
-
-        @pl.when(has_up)
-        def _():
-            side_rows(up, 0, part, cam).start()
-
-        @pl.when(has_down)
-        def _():
-            side_rows(down, 1, part, cam).start()
-
+    for copy in bias_in:
+        copy.wait()
+    bias_ref[...] = jnp.concatenate([bias_rows[i] for i in range(bias_rows.shape[0])], axis=1)
     own_cells.wait()
     cell_copy(mate, 1 - cam, 0, cam).wait_recv()
 
@@ -475,6 +488,30 @@
 
     def wait_for(name):
         if name == "own":
+            kept.wait()
+
+            @pl.loop(0, count_y)
+            def _(step):
+                part = (bevy + step) % count_y
+
+                @pl.loop(0, count_x)
+                def _(index):
+                    source = part * count_x + index
+
+                    @pl.when(source != me)
+                    def _():
+                        tile_copy(source, source).wait_recv()
+
+                mate_rows(part, cam).start()
+
+                @pl.when(has_up)
+                def _():
+                    side_rows(up, 0, part, cam).start()
+
+                @pl.when(has_down)
+                def _():
+                    side_rows(down, 1, part, cam).start()
+
 
             @pl.loop(0, count_y)
             def _(part):
@@ -498,7 +535,6 @@
         for copy in {"lift": copies[:1], "qkv": copies[1:4], "out": copies[4:]}[name]:
             copy.wait()
 
-    row_start = (bevy * 2 + cam) * ROWS_DEV
     cells_own = jnp.concatenate([cells[0, 0:1, :], cells[1, 0:1, :]], axis=1)
     cells_side = jnp.concatenate([cells[2, 0:1, :], cells[3, 0:1, :]], axis=1)
     slot_attention(
@@ -542,14 +578,6 @@
     heads = key_bias.shape[2]
     grid_rows = key_bias.shape[0]
     half = image_tokens.shape[1] // 2
-    live = lax.broadcasted_iota(jnp.int32, (tile_count, slot_count), 1) < slot_counts[0, 0][:, None]
-    wanted = jnp.where(live, route_token[0, 0], -1)[:, None, :]
-    wanted = jnp.broadcast_to(wanted, (tile_count, 2, slot_count)).reshape(1, -1)
-    cells = jnp.broadcast_to(route_cell.reshape(1, -1), (8, tile_count * slot_count))
-    row_start = lax.axis_index(("bevy", "cam")) * ROWS_DEV
-    padded = jnp.pad(key_bias, ((HALO, HALO), (0, 0), (0, 0)))
-    window = lax.dynamic_slice_in_dim(padded, row_start, 2 * ROWS_DEV, 0)
-    window = window.reshape(-1, heads).T
     slots = 2 * tile_count * slot_count
     vmem = pl.BlockSpec(memory_space=pltpu.VMEM)
     anywhere = pl.BlockSpec(memory_space=pl.ANY)
@@ -559,16 +587,20 @@
     out = pl.pallas_call(
         functools.partial(fused_kernel, grid_rows),
         out_shape=jax.ShapeDtypeStruct((ROWS_DEV * COLS_DEV, width), jnp.bfloat16),
-        in_specs=[vmem] * 5 + [anywhere] * 5,
+        in_specs=[vmem] * 4 + [anywhere] * 7,
         out_specs=vmem,
         scratch_shapes=[pltpu.VMEM(w.shape, jnp.bfloat16) for w in weights]
         + [
             dma((5,)),
             pltpu.VMEM((slots, half), jnp.bfloat16),
             pltpu.VMEM((4, slots, half), jnp.bfloat16),
-            pltpu.VMEM((4,) + cells.shape, jnp.int32),
+            pltpu.VMEM((4, 8, slots // 2), jnp.int32),
             pltpu.VMEM((2 * slots, 2 * half), jnp.bfloat16),
-            dma((2,)),
+            pltpu.VMEM(image_tokens.shape, jnp.bfloat16),
+            pltpu.VMEM((2 * ROWS_DEV, heads, COLS_DEV), jnp.bfloat16),
+            pltpu.VMEM((8, slots // 2), jnp.int32),
+            pltpu.VMEM((heads, 2 * ROWS_DEV * COLS_DEV), jnp.bfloat16),
+            dma((6,)),
             dma((tile_count,)),
             dma((tile_count,)),
             dma((count_y,)),
@@ -580,9 +612,17 @@
         ]
         + compute_scratch(slots, heads, width),
         compiler_params=pltpu.CompilerParams(
-            vmem_limit_bytes=48 * 2**20, collective_id=0, has_side_effects=True
+            vmem_limit_bytes=62 * 2**20, collective_id=0, has_side_effects=True
         ),
-    )(wanted, cells, image_tokens, window, norm_gain.reshape(1, -1), *weights)
+    )(
+        route_token[0, 0].T,
+        route_cell[:, 0, 0, :].T,
+        slot_counts.reshape(1, -1),
+        norm_gain.reshape(1, -1),
+        image_tokens,
+        key_bias.transpose(0, 2, 1),
+        *weights,
+    )
     return out.reshape(ROWS_DEV, COLS_DEV, width)
 
 

time: 43.9 us -> 40.3 us (0.918)
  local copies, waits for them, and re-layouts: 7.68 us -> 2.26 us
  Pallas kernels: 35.1 us -> 37.9 us
  other arithmetic: 0.69 us -> 0 us
    unnamed x10 -> x1, local copies, waits for them, and re-layouts: 6.41 us -> 2.26 us
    pallas_call x1, Pallas kernels: 35.1 us -> 37.9 us  [slot_body(): pl.pallas_call(functools.partial(fused_kernel, grid_rows), out_shape=jax....]
    dynamic_slice x2 -> x0, local copies, waits for them, and re-layouts: 0.89 us -> none  [slot_body(): window = lax.dynamic_slice_in_dim(padded, row_start, 2 * ROWS_DEV, 0)]
    select_n x1 -> x0, other arithmetic: 0.69 us -> none  [slot_body(): wanted = jnp.where(live, route_token[0, 0], -1)[:, None, :]]
where the time goes in v3:
time: 40.3 us; the launch traced here: 40.1 us
  Pallas kernels  37.9 us (94%)
  local copies, waits for them, and re-layouts  2.26 us (6%)
    pallas_call x1, Pallas kernels, slot_body(): pl.pallas_call(functools.partial(fused_kernel, grid_rows), out_shape=jax....  37.9 us
    unnamed x1, local copies, waits for them, and re-layouts  2.26 us

profile of v3, /device:TPU:1, one launch (start us, length us, event | category | flops | bytes accessed | tf_op | source)
XLA Modules:
  0.0 40.1 jit_solution(10564387132042863100)
XLA Ops:
  0.0 37.9 %shard_map.109 = bf16[512,1024]{1,0:T(8,128)(2,1)} custom-call(s32[8,16]{1,0:T(8,128)} %bitcast.12, s32[8,16]{1,0:T(8,128)} %bitcast.13, s32[1,16]{1,0:T(1,128)} %bitcast.15, f32[1,1024]{1,0:T(1,128)} %bitcast.14, bf16[256,768]{1,0:T(8,128)(2,1)} %tokens_h.1, bf16[64,16,64]{2,1,0:T(8,128)(2,1)} %bitcast.11, bf16[768,1024]{1,0:T(8,128)(2,1)} %lift_h.1, ...), custom_call_target="tpu_custom_call" | custom-call | tf_op jit(solution)/shard_map/pallas_call | solution.py:587
  37.9 2.3 %copy.13 = bf16[8,64,1024]{2,1,0:T(8,128)(2,1)} copy(bf16[8,64,1024]{2,1,0:T(8,128)(2,1)} %bitcast.10) | data formatting | bytes 2097152

commit v4 on v3

--- a/solution.py
+++ b/solution.py
@@ -257,10 +257,10 @@
 
     low = lax.broadcasted_iota(jnp.int32, (slots, 2 * head_size), 1) < head_size
 
-    @pl.loop(0, heads // 4)
+    @pl.loop(0, heads // 16)
     def _(step):
-        for inner in range(2):
-            pair = step * 2 + inner
+        for inner in range(8):
+            pair = step * 8 + inner
             cols = pl.ds(pl.multiple_of(pair * 2 * head_size, 2 * head_size), 2 * head_size)
             query = queries[:, cols]
             parts = []

time: 40.3 us -> 39.9 us (0.990)
  Pallas kernels: 37.9 us -> 37.4 us
    pallas_call x1, Pallas kernels: 37.9 us -> 37.4 us  [slot_body(): pl.pallas_call(functools.partial(fused_kernel, grid_rows), out_shape=jax....]
where the time goes in v4:
time: 39.9 us; the launch traced here: 39.7 us
  Pallas kernels  37.4 us (94%)
  local copies, waits for them, and re-layouts  2.26 us (6%)
    pallas_call x1, Pallas kernels, slot_body(): pl.pallas_call(functools.partial(fused_kernel, grid_rows), out_shape=jax....  37.4 us
    unnamed x1, local copies, waits for them, and re-layouts  2.26 us

profile of v4, /device:TPU:1, one launch (start us, length us, event | category | flops | bytes accessed | tf_op | source)
XLA Modules:
  0.0 39.7 jit_solution(2252120734380545332)
XLA Ops:
  0.0 37.4 %shard_map.109 = bf16[512,1024]{1,0:T(8,128)(2,1)} custom-call(s32[8,16]{1,0:T(8,128)} %bitcast.12, s32[8,16]{1,0:T(8,128)} %bitcast.13, s32[1,16]{1,0:T(1,128)} %bitcast.15, f32[1,1024]{1,0:T(1,128)} %bitcast.14, bf16[256,768]{1,0:T(8,128)(2,1)} %tokens_h.1, bf16[64,16,64]{2,1,0:T(8,128)(2,1)} %bitcast.11, bf16[768,1024]{1,0:T(8,128)(2,1)} %lift_h.1, ...), custom_call_target="tpu_custom_call" | custom-call | tf_op jit(solution)/shard_map/pallas_call | solution.py:587
  37.4 2.3 %copy.13 = bf16[8,64,1024]{2,1,0:T(8,128)(2,1)} copy(bf16[8,64,1024]{2,1,0:T(8,128)(2,1)} %bitcast.10) | data formatting | bytes 2097152
